TPU v7x, 128 devices: a whole 4x4x4 slice. The times are simulated.
128 devices in a mesh: row: 8 (over z, core), col: 16 (over x, y).
Axes of the slice: x: 4, y: 4, z: 4, core: 2. Of those that a mesh axis runs over, the one named last changes fastest.
Arguments:
- compound_pos: float32 [32768, 128], P(('row', 'col')), may hold values from -1.75 to 1.75
- compound_mom: float32 [32768, 128], P(('row', 'col')), may hold values from -6 to 6
- target_pos: float32 [32768, 128], P(('row', 'col')), may hold values from -1.75 to 1.75
- target_mom: float32 [32768, 128], P(('row', 'col')), may hold values from -6 to 6
- tile_rows: int32 [128, 256], P(('row', 'col')), may hold values from 0 to 255, as said below
- tile_cols: int32 [128, 256], P(('row', 'col')), may hold values from 0 to 255, as said below
- tile_count: int32 [128], P(('row', 'col')), may hold values from 32 to 256, as said below
- tile_values: bfloat16 [128, 256, 128, 128], P(('row', 'col')), may hold values from -6 to 6
- tile_weight: bfloat16 [128, 256, 128, 128], P(('row', 'col')), may hold values from 0 to 2, as said below
Outputs:
- compound_out: float32 [32768, 128], P(('row', 'col'))
- compound_mom_out: float32 [32768, 128], P(('row', 'col'))
- target_out: float32 [32768, 128], P(('row', 'col'))
- target_mom_out: float32 [32768, 128], P(('row', 'col'))
Inputs may be any that keep to these rules, and one draw needn't show every extreme that they name: `tile_rows`: slots of device d = i * 16 + j name compound blocks from i * 16 * 2 to (i + 1) * 16 * 2 - 1. `tile_cols`: slots of device d = i * 16 + j name target blocks (a * 16 + j) * 2 + c with a < 8 and c < 2. `tile_count`: some device has all 256 slots live in every draw. `tile_weight`: unobserved entries are 0; observed ones are positive.
All inputs are finite; a program needn't handle non-finite values.
Results may differ from a plain program's by a relative error of at most 0.0095.
Values may be sent and summed in bfloat16 or wider, within the bound.
A program may use at most 128 MiB of HBM per device.

v0:
```python
import math

import jax
import jax.numpy as jnp
from jax import lax
from jax.sharding import PartitionSpec as P

LEAPS = 2


degrees_free = 4.0
noise_scale = 0.5
prior_weight = 1.0
step_size = 0.01


def tile_terms(comp_rows, targ_rows, values, entry_weight, alive_mask):
    predicted = jnp.einsum("tik,tjk->tij", comp_rows, targ_rows, preferred_element_type=jnp.float32)
    resid_tile = values.astype(jnp.float32) - predicted
    weights = (
        (degrees_free + 1.0)
        * resid_tile
        / (degrees_free * noise_scale * noise_scale + resid_tile * resid_tile)
    )
    kept_mask = entry_weight.astype(jnp.float32) * alive_mask[:, None, None]
    scaled = (weights * kept_mask).astype(jnp.bfloat16)
    comp_part = jnp.einsum("tij,tjk->tik", scaled, targ_rows, preferred_element_type=jnp.float32)
    targ_part = jnp.einsum("tij,tik->tjk", scaled, comp_rows, preferred_element_type=jnp.float32)
    return (comp_part, targ_part)


def leapfrog(places, speeds, force_fn):
    comp_place, targ_place = places
    comp_speed, targ_speed = speeds
    comp_force, targ_force = force_fn(comp_place, targ_place)
    for leap_index in range(LEAPS):
        comp_speed = comp_speed + 0.5 * step_size * comp_force
        targ_speed = targ_speed + 0.5 * step_size * targ_force
        comp_place = comp_place + step_size * comp_speed
        targ_place = targ_place + step_size * targ_speed
        comp_force, targ_force = force_fn(comp_place, targ_place)
        comp_speed = comp_speed + 0.5 * step_size * comp_force
        targ_speed = targ_speed + 0.5 * step_size * targ_force
    return (comp_place, comp_speed, targ_place, targ_speed)


def body(
    compound_pos,
    compound_mom,
    target_pos,
    target_mom,
    tile_rows,
    tile_cols,
    tile_count,
    tile_values,
    tile_weight,
):
    tile_side = tile_values.shape[2]
    rank_width = compound_pos.shape[1]
    comp_local_blocks = compound_pos.shape[0] // tile_side
    targ_local_blocks = target_pos.shape[0] // tile_side
    col_devs = lax.axis_size("col")
    row_devs = lax.axis_size("row")
    row_index = lax.axis_index("row")
    slot_count = tile_values.shape[1]
    batch_size = math.gcd(slot_count, 32)
    rounds = slot_count // batch_size
    comp_group = col_devs * comp_local_blocks
    targ_group = row_devs * targ_local_blocks
    row_local = tile_rows[0] - row_index * comp_group
    col_holder = tile_cols[0] // targ_local_blocks
    col_local = col_holder // col_devs * targ_local_blocks + tile_cols[0] % targ_local_blocks
    alive_all = (jnp.arange(slot_count, dtype=jnp.int32) < tile_count[0]).astype(jnp.float32)
    batches = (
        tile_values[0].reshape(rounds, batch_size, tile_side, tile_side),
        tile_weight[0].reshape(rounds, batch_size, tile_side, tile_side),
        row_local.reshape(rounds, batch_size),
        col_local.reshape(rounds, batch_size),
        alive_all.reshape(rounds, batch_size),
    )

    def local_grads(comp_low, targ_low):
        comp_tiles = comp_low.reshape(comp_group, tile_side, rank_width)
        targ_tiles = targ_low.reshape(targ_group, tile_side, rank_width)

        def visit(carry, pieces):
            values, entry_weight, row_ids, col_ids, alive_mask = pieces
            comp_part, targ_part = tile_terms(
                comp_tiles[row_ids], targ_tiles[col_ids], values, entry_weight, alive_mask
            )
            comp_acc = carry[0].at[row_ids].add(comp_part)
            targ_acc = carry[1].at[col_ids].add(targ_part)
            return ((comp_acc, targ_acc), None)

        start = (
            jnp.zeros((comp_group, tile_side, rank_width), jnp.float32),
            jnp.zeros((targ_group, tile_side, rank_width), jnp.float32),
        )
        (comp_acc, targ_acc), unused = lax.scan(visit, start, batches)
        return (
            comp_acc.reshape(comp_group * tile_side, rank_width),
            targ_acc.reshape(targ_group * tile_side, rank_width),
        )

    def owner_forces(comp_now, targ_now):
        comp_low = lax.all_gather(comp_now.astype(jnp.bfloat16), "col", axis=0, tiled=True)
        targ_low = lax.all_gather(targ_now.astype(jnp.bfloat16), "row", axis=0, tiled=True)
        comp_acc, targ_acc = local_grads(comp_low, targ_low)
        comp_sum = lax.psum_scatter(
            comp_acc.astype(jnp.bfloat16), "col", scatter_dimension=0, tiled=True
        ).astype(jnp.float32)
        targ_sum = lax.psum_scatter(
            targ_acc.astype(jnp.bfloat16), "row", scatter_dimension=0, tiled=True
        ).astype(jnp.float32)
        return (comp_sum - prior_weight * comp_now, targ_sum - prior_weight * targ_now)

    return leapfrog((compound_pos, target_pos), (compound_mom, target_mom), owner_forces)


def solution(mesh):
    return jax.shard_map(
        body,
        mesh=mesh,
        in_specs=(
            P(("row", "col"), None),
            P(("row", "col"), None),
            P(("row", "col"), None),
            P(("row", "col"), None),
            P(("row", "col"), None),
            P(("row", "col"), None),
            P(("row", "col")),
            P(("row", "col"), None, None, None),
            P(("row", "col"), None, None, None),
        ),
        out_specs=(
            P(("row", "col"), None),
            P(("row", "col"), None),
            P(("row", "col"), None),
            P(("row", "col"), None),
        ),
        check_vma=False,
    )
```

profile of v0, /device:TPU:1, one launch (start us, length us, event | category | flops | bytes accessed | tf_op | source)
XLA Modules:
  0.0 993.0 jit_solution(6318859090897908695)
XLA Ops:
  13.7 16.7 %all_gather.19 = bf16[2048,128]{1,0:T(8,128)(2,1)} all-gather(bf16[256,128]{1,0:T(8,128)(2,1)S(1)} %convert_element_type.122), channel_id=1, replica_groups=mesh['row'=8,'col'=16] {'row'}, dimensions={0}, use_global_device_ids=true | all-gather | bytes 589824 | tf_op jit(solution)/shard_map/all_gather | solution.py:107
  30.4 24.7 %all-gather.4.cloned.1.call-done = bf16[4096,128]{1,0:T(8,128)(2,1)} async-done(((bf16[256,128]{1,0:T(8,128)(2,1)}), bf16[4096,128]{1,0:T(8,128)(2,1)}) %all-gather.4.cloned.1.call-update) | async-done | bytes 1048592 | tf_op jit(solution)/shard_map/all_gather | solution.py:106
  56.8 171.0 %while.36 = (s32[]{:T(128)}, f32[32,128,128]{2,1,0:T(8,128)}, f32[16,128,128]{2,1,0:T(8,128)S(1)}, s32[8,32]{1,0:T(8,128)S(1)}, bf16[8,32,128,128]{3,2,1,0:T(8,1...) while((s32[]{:T(128)}, f32[32,128,128]{2,1,0:T(8,128)}, ...), condition=%wide.region_3.4_spmd, body=%wide.region_0.3_spmd.sunk | while | flops 408946880 | bytes 43001676 | solution.py:99
  67.4 2.7 scatter_fusion.1
  72.0 6.2 scatter_fusion
  88.8 2.7 scatter_fusion.1
  93.5 6.1 scatter_fusion
  114.8 6.1 scatter_fusion
  136.1 6.2 scatter_fusion
  157.6 6.2 scatter_fusion
  174.4 2.7 scatter_fusion.1
  179.0 6.1 scatter_fusion
  200.4 6.1 scatter_fusion
  221.7 6.0 scatter_fusion
  228.4 2.7 convert_element_type.124
  232.2 71.3 %reduce-scatter.7.cloned.1.call-done = bf16[256,128]{1,0:T(8,128)(2,1)} async-done(((bf16[4096,128]{1,0:T(8,128)(2,1)}), bf16[256,128]{1,0:T(8,128)(2,1)}) %reduce-scatter.7.cloned.1.call-update) | async-done | bytes 65552 | tf_op jit(solution)/shard_map/reduce_scatter | solution.py:109
  305.1 30.1 %reduce-scatter.9.cloned.1.call-done = bf16[256,128]{1,0:T(8,128)(2,1)} async-done(((bf16[2048,128]{1,0:T(8,128)(2,1)}), bf16[256,128]{1,0:T(8,128)(2,1)}) %reduce-scatter.9.cloned.1.call-update) | async-done | bytes 65552 | tf_op jit(solution)/shard_map/reduce_scatter | solution.py:112
  336.1 17.6 %all_gather.21 = bf16[2048,128]{1,0:T(8,128)(2,1)} all-gather(bf16[256,128]{1,0:T(8,128)(2,1)S(1)} %fusion.22), channel_id=1, replica_groups=mesh['row'=8,'col'=16] {'row'}, dimensions={0}, use_global_device_ids=true | all-gather | bytes 589824 | tf_op jit(solution)/shard_map/all_gather | solution.py:107
  353.7 26.9 %all-gather.6.cloned.1.call-done = bf16[4096,128]{1,0:T(8,128)(2,1)} async-done(((bf16[256,128]{1,0:T(8,128)(2,1)}), bf16[4096,128]{1,0:T(8,128)(2,1)}) %all-gather.6.cloned.1.call-update) | async-done | bytes 1048592 | tf_op jit(solution)/shard_map/all_gather | solution.py:106
  382.3 171.0 %while.37 = (s32[]{:T(128)}, f32[32,128,128]{2,1,0:T(8,128)}, f32[16,128,128]{2,1,0:T(8,128)S(1)}, s32[8,32]{1,0:T(8,128)S(1)}, bf16[8,32,128,128]{3,2,1,0:T(8,1...) while((s32[]{:T(128)}, f32[32,128,128]{2,1,0:T(8,128)}, ...), condition=%wide.region_9.10_spmd, body=%wide.region_6.9_spmd.sunk | while | flops 408946880 | bytes 43001676 | solution.py:99
  392.9 2.7 scatter_fusion.3
  397.6 6.2 scatter_fusion.2
  414.4 2.7 scatter_fusion.3
  419.0 6.1 scatter_fusion.2
  440.4 6.1 scatter_fusion.2
  461.7 6.2 scatter_fusion.2
  483.2 6.2 scatter_fusion.2
  504.6 6.1 scatter_fusion.2
  525.9 6.1 scatter_fusion.2
  547.3 6.0 scatter_fusion.2
  553.3 2.7 convert_element_type.132
  557.1 71.4 %reduce-scatter.11.cloned.1.call-done = bf16[256,128]{1,0:T(8,128)(2,1)} async-done(((bf16[4096,128]{1,0:T(8,128)(2,1)}), bf16[256,128]{1,0:T(8,128)(2,1)}) %reduce-scatter.11.cloned.1.call-update) | async-done | bytes 65552 | tf_op jit(solution)/shard_map/reduce_scatter | solution.py:109
  630.1 29.9 %reduce-scatter.13.cloned.1.call-done = bf16[256,128]{1,0:T(8,128)(2,1)} async-done(((bf16[2048,128]{1,0:T(8,128)(2,1)}), bf16[256,128]{1,0:T(8,128)(2,1)}) %reduce-scatter.13.cloned.1.call-update) | async-done | bytes 65552 | tf_op jit(solution)/shard_map/reduce_scatter | solution.py:112
  661.6 17.8 %all_gather.23 = bf16[2048,128]{1,0:T(8,128)(2,1)} all-gather(bf16[256,128]{1,0:T(8,128)(2,1)S(1)} %get-tuple-element.229), channel_id=1, replica_groups=mesh['row'=8,'col'=16] {'row'}, dimensions={0}, use_global_device_ids=true | all-gather | bytes 589824 | tf_op jit(solution)/shard_map/all_gather | solution.py:107
  679.4 26.1 %all-gather.8.cloned.1.call-done = bf16[4096,128]{1,0:T(8,128)(2,1)} async-done(((bf16[256,128]{1,0:T(8,128)(2,1)}), bf16[4096,128]{1,0:T(8,128)(2,1)}) %all-gather.8.cloned.1.call-update) | async-done | bytes 1048592 | tf_op jit(solution)/shard_map/all_gather | solution.py:106
  707.2 171.0 %while.38 = (s32[]{:T(128)}, f32[32,128,128]{2,1,0:T(8,128)}, f32[16,128,128]{2,1,0:T(8,128)S(1)}, s32[8,32]{1,0:T(8,128)S(1)}, bf16[8,32,128,128]{3,2,1,0:T(8,1...) while((s32[]{:T(128)}, f32[32,128,128]{2,1,0:T(8,128)}, ...), condition=%wide.region_15.16_spmd, body=%wide.region_12.15_spmd.sunk | while | flops 408946880 | bytes 43001676 | solution.py:99
  717.8 2.7 scatter_fusion.5
  722.4 6.2 scatter_fusion.4
  739.2 2.7 scatter_fusion.5
  743.9 6.1 scatter_fusion.4
  765.2 6.1 scatter_fusion.4
  786.5 6.2 scatter_fusion.4
  808.0 6.2 scatter_fusion.4
  829.4 6.1 scatter_fusion.4
  850.8 6.1 scatter_fusion.4
  872.1 6.0 scatter_fusion.4
  881.2 27.3 %reduce-scatter.17.cloned.1.call-done = bf16[256,128]{1,0:T(8,128)(2,1)} async-done(((bf16[2048,128]{1,0:T(8,128)(2,1)}), bf16[256,128]{1,0:T(8,128)(2,1)}) %reduce-scatter.17.cloned.1.call-update) | async-done | bytes 65552 | tf_op jit(solution)/shard_map/reduce_scatter | solution.py:112
  910.0 74.8 %reduce-scatter.15.cloned.1.call-done = bf16[256,128]{1,0:T(8,128)(2,1)} async-done(((bf16[4096,128]{1,0:T(8,128)(2,1)}), bf16[256,128]{1,0:T(8,128)(2,1)}) %reduce-scatter.15.cloned.1.call-update) | async-done | bytes 65552 | tf_op jit(solution)/shard_map/reduce_scatter | solution.py:109
  (452 shorter events, 370.1 us)
Async XLA Ops:
  7.2 47.9 %all-gather.4.cloned.1.call-start = ((), (), s32[]{:S(2)}) async-start(), calls=%async_computation.6 | async-start | bytes 1114112 | tf_op jit(solution)/shard_map/all_gather | solution.py:106
  8.8 294.7 %reduce-scatter.7.cloned.1.call-start = ((), (), s32[]{:S(2)}) async-start(), calls=%async_computation.7 | async-start | bytes 1114112 | tf_op jit(solution)/shard_map/reduce_scatter | solution.py:109
  59.5 2.2 copy-start.3
  80.9 2.2 copy-start.3
  102.3 2.2 copy-start.3
  123.6 2.2 copy-start.3
  145.1 2.2 copy-start.3
  166.5 2.2 copy-start.3
  187.8 2.2 copy-start.3
  209.2 2.2 copy-start.3
  231.1 72.4 %copy-start.11 = (f32[256,128]{1,0:T(8,128)S(1)}, f32[256,128]{1,0:T(8,128)}, u32[]{:S(2)}) copy-start(f32[256,128]{1,0:T(8,128)} %param.15) | copy-start | bytes 393220
  231.1 72.4 %copy-start.13 = (f32[256,128]{1,0:T(8,128)S(1)}, f32[256,128]{1,0:T(8,128)}, u32[]{:S(2)}) copy-start(f32[256,128]{1,0:T(8,128)} %param.16) | copy-start | bytes 393220
  231.1 104.1 %copy-start.10 = (f32[256,128]{1,0:T(8,128)S(1)}, f32[256,128]{1,0:T(8,128)}, u32[]{:S(2)}) copy-start(f32[256,128]{1,0:T(8,128)} %param.17) | copy-start | bytes 393220
  231.1 104.1 %copy-start.12 = (f32[256,128]{1,0:T(8,128)S(1)}, f32[256,128]{1,0:T(8,128)}, u32[]{:S(2)}) copy-start(f32[256,128]{1,0:T(8,128)} %param.18) | copy-start | bytes 393220
  231.1 104.1 %reduce-scatter.9.cloned.1.call-start = ((), (), s32[]{:S(2)}) async-start(), calls=%async_computation.9 | async-start | bytes 589824 | tf_op jit(solution)/shard_map/reduce_scatter | solution.py:112
  232.1 148.5 %all-gather.6.cloned.1.call-start = ((), (), s32[]{:S(2)}) async-start(), calls=%async_computation.8 | async-start | bytes 1114112 | tf_op jit(solution)/shard_map/all_gather | solution.py:106
  305.1 323.4 %reduce-scatter.11.cloned.1.call-start = ((), (), s32[]{:S(2)}) async-start(), calls=%async_computation.10 | async-start | bytes 1114112 | tf_op jit(solution)/shard_map/reduce_scatter | solution.py:109
  385.0 2.9 copy-start.4
  406.4 2.9 copy-start.4
  427.8 2.9 copy-start.4
  449.1 2.9 copy-start.4
  470.6 2.9 copy-start.4
  492.0 2.9 copy-start.4
  513.4 2.9 copy-start.4
  519.1 2.2 copy-start.7
  534.7 2.9 copy-start.4
  556.0 72.4 %copy-start.14 = (f32[256,128]{1,0:T(8,128)S(1)}, f32[256,128]{1,0:T(8,128)}, u32[]{:S(2)}) copy-start(f32[256,128]{1,0:T(8,128)} %param.16) | copy-start | bytes 393220
  556.1 72.4 %copy-start.16 = (bf16[256,128]{1,0:T(8,128)(2,1)S(1)}, bf16[256,128]{1,0:T(8,128)(2,1)}, u32[]{:S(2)}) copy-start(bf16[256,128]{1,0:T(8,128)(2,1)} %reduce-scatter.7.cloned.1.call-done) | copy-start | bytes 196612
  556.1 104.0 %copy-start.18 = (bf16[256,128]{1,0:T(8,128)(2,1)S(1)}, bf16[256,128]{1,0:T(8,128)(2,1)}, u32[]{:S(2)}) copy-start(bf16[256,128]{1,0:T(8,128)(2,1)} %reduce-scatter.9.cloned.1.call-done) | copy-start | bytes 196612
  556.1 103.9 %reduce-scatter.13.cloned.1.call-start = ((), (), s32[]{:S(2)}) async-start(), calls=%async_computation.12 | async-start | bytes 589824 | tf_op jit(solution)/shard_map/reduce_scatter | solution.py:112
  557.1 148.4 %all-gather.8.cloned.1.call-start = ((), (), s32[]{:S(2)}) async-start(), calls=%async_computation.11 | async-start | bytes 1114112 | tf_op jit(solution)/shard_map/all_gather | solution.py:106
  630.1 278.4 %reduce-scatter.17.cloned.1.call-start = ((), (), s32[]{:S(2)}) async-start(), calls=%async_computation.14 | async-start | bytes 589824 | tf_op jit(solution)/shard_map/reduce_scatter | solution.py:112
  709.9 2.9 copy-start.5
  731.3 2.9 copy-start.5
  752.6 2.9 copy-start.5
  774.0 2.9 copy-start.5
  795.4 2.9 copy-start.5
  816.9 2.9 copy-start.5
  838.2 2.9 copy-start.5
  859.6 2.9 copy-start.5
  879.1 105.8 %reduce-scatter.15.cloned.1.call-start = ((), (), s32[]{:S(2)}) async-start(), calls=%async_computation.13 | async-start | bytes 1114112 | tf_op jit(solution)/shard_map/reduce_scatter | solution.py:109
  879.9 28.5 %copy-start.19 = (bf16[256,128]{1,0:T(8,128)(2,1)S(1)}, bf16[256,128]{1,0:T(8,128)(2,1)}, u32[]{:S(2)}) copy-start(bf16[256,128]{1,0:T(8,128)(2,1)} %reduce-scatter.9.cloned.1.call-done) | copy-start | bytes 196612
  879.9 28.5 %copy-start.21 = (f32[256,128]{1,0:T(8,128)S(1)}, f32[256,128]{1,0:T(8,128)}, u32[]{:S(2)}) copy-start(f32[256,128]{1,0:T(8,128)} %get-tuple-element.230) | copy-start | bytes 393220
  879.9 28.5 %copy-start.23 = (bf16[256,128]{1,0:T(8,128)(2,1)S(1)}, bf16[256,128]{1,0:T(8,128)(2,1)}, u32[]{:S(2)}) copy-start(bf16[256,128]{1,0:T(8,128)(2,1)} %reduce-scatter.13.cloned.1.call-done) | copy-start | bytes 196612
  880.0 104.9 %copy-start.15 = (f32[256,128]{1,0:T(8,128)S(1)}, f32[256,128]{1,0:T(8,128)}, u32[]{:S(2)}) copy-start(f32[256,128]{1,0:T(8,128)} %param.16) | copy-start | bytes 393220
  880.0 104.9 %copy-start.17 = (bf16[256,128]{1,0:T(8,128)(2,1)S(1)}, bf16[256,128]{1,0:T(8,128)(2,1)}, u32[]{:S(2)}) copy-start(bf16[256,128]{1,0:T(8,128)(2,1)} %reduce-scatter.7.cloned.1.call-done) | copy-start | bytes 196612
  880.0 104.9 %copy-start.20 = (f32[256,128]{1,0:T(8,128)S(1)}, f32[256,128]{1,0:T(8,128)}, u32[]{:S(2)}) copy-start(f32[256,128]{1,0:T(8,128)} %get-tuple-element.232) | copy-start | bytes 393220
  880.0 104.9 %copy-start.22 = (bf16[256,128]{1,0:T(8,128)(2,1)S(1)}, bf16[256,128]{1,0:T(8,128)(2,1)}, u32[]{:S(2)}) copy-start(bf16[256,128]{1,0:T(8,128)(2,1)} %reduce-scatter.11.cloned.1.call-done) | copy-start | bytes 196612
  (49 other events, 75.2 us)
Sparse Core Ops, SparseCore 0:
  10.7 44.3 all-gather.3
  231.3 72.2 reduce-scatter.6
  306.0 29.1 reduce-scatter.8
  337.8 42.7 all-gather.5
  556.2 72.2 reduce-scatter.10
  630.8 29.1 reduce-scatter.12
  662.7 42.7 all-gather.7
  879.2 29.1 reduce-scatter.16
  912.0 72.8 reduce-scatter.14
where the time goes:
time: 1000 us; the launch traced here: 993 us
  waiting for transfers between devices  383 us (38%)
  other arithmetic  251 us (25%)
  matrix products  160 us (16%)
  local copies, waits for them, and re-layouts  130 us (13%)
  blocking collectives  52.1 us (5%)
  between operations  14.6 us (1%)
    reduce_scatter x3, waiting for transfers between devices, owner_forces(): lax.psum_scatter(comp_acc.astype(jnp.bfloat16), 'col', scatter_dimension=...  218 us
    scatter-add x24, other arithmetic, visit(): comp_acc = carry[0].at[row_ids].add(comp_part)  147 us
    reduce_scatter x3, waiting for transfers between devices, owner_forces(): lax.psum_scatter(targ_acc.astype(jnp.bfloat16), 'row', scatter_dimension=...  87.3 us
    all_gather x3, waiting for transfers between devices, owner_forces(): lax.all_gather(comp_now.astype(jnp.bfloat16), 'col', axis=0, tiled=True)  77.7 us
    scatter-add x24, other arithmetic, visit(): targ_acc = carry[1].at[col_ids].add(targ_part)  64 us
    dot_general x24, matrix products, tile_terms(): jnp.einsum('tik,tjk->tij', comp_rows, targ_rows, preferred_element_type=j...  61.8 us
    all_gather x3, blocking collectives, owner_forces(): lax.all_gather(targ_now.astype(jnp.bfloat16), 'row', axis=0, tiled=True)  52.1 us
    gather x24, local copies, waits for them, and re-layouts, visit(): targ_tiles[col_ids]  51.9 us
  transfers between devices with their start and end apart: 9, of which 9 were waited for; matrix products, arithmetic and copies ran while one was open for 1% of the time, Pallas kernels for 0%

commit v1 on v0

v1 whole, which is shorter than its diff:
```python
import functools

import jax
import jax.numpy as jnp
from jax import lax
from jax.experimental import pallas as pl
from jax.experimental.pallas import tpu as pltpu
from jax.sharding import PartitionSpec as P

MESH = pl.DeviceIdType.MESH
BF = jnp.bfloat16
F32 = jnp.float32
NT = (((1,), (1,)), ((), ()))

LEAPS = 2
EPS = 0.01
LAMBDA = 1.0
NU1 = 5.0
NU_S2 = 1.0
GROUP = 8


def plan(local, live, blocks, cap):
    slots = local.shape[0]
    hit = (local[:, None] == jnp.arange(blocks)[None, :]) & live[:, None]
    hits = hit.astype(jnp.int32)
    count = hits.sum(0)
    pairs = (count + 1) // 2
    ids = jnp.arange(blocks)
    start = jnp.where(ids[None, :] < ids[:, None], pairs[None, :], 0).sum(1)
    earlier = jnp.arange(slots)[None, :] < jnp.arange(slots)[:, None]
    same = (local[None, :] == local[:, None]) & live[None, :]
    rank = (earlier & same).astype(jnp.int32).sum(1)
    place = jnp.where(live, 2 * (hits * start[None, :]).sum(1) + rank, 2 * cap)
    pair_ids = jnp.arange(cap)
    inside = (pair_ids[:, None] >= start[None, :]) & (
        pair_ids[:, None] < (start + pairs)[None, :]
    )
    block = (inside * ids[None, :]).sum(1).astype(jnp.int32)
    first = (inside & (pair_ids[:, None] == start[None, :])).any(1)
    keep = jnp.where(first, 0, 1).astype(jnp.int32)
    last = jnp.where(count > 0, start + pairs - 1, 0).astype(jnp.int32)
    some = (count > 0).astype(jnp.int32)
    at = place[None, :] == jnp.arange(2 * cap)[:, None]
    return place, at, block, keep, last, some


def pick(at, values, default):
    hit = at.any(1)
    got = (at * values[None, :]).sum(1)
    return jnp.where(hit, got, default).astype(jnp.int32)


def kernel(
    sizes,
    ua_ref, uslot_ref, ub_ref, ukeep_ref, ulast_ref, usome_ref,
    va_ref, vpos_ref, vkeep_ref, vlast_ref, vsome_ref,
    upos_ref, umom_ref, vpos0_ref, vmom_ref, vals_hbm, wts_hbm,
    uq_ref, up_ref, vq_ref, vp_ref,
    vals, wts, wgt, part, u_all, ut_all, v_all, u_own, v_own,
    u_send, u_recv, v_send, v_recv,
    load_sem, agu_s, agu_r, agv_s, agv_r, rsu_s, rsu_r, rsv_s, rsv_r,
):
    rows, cols, slots, bs, upairs, vpairs = sizes
    r = lax.axis_index("row")
    c = lax.axis_index("col")

    loads = (
        pltpu.make_async_copy(vals_hbm, vals.at[pl.ds(0, slots)], load_sem.at[0]),
        pltpu.make_async_copy(wts_hbm, wts.at[pl.ds(0, slots)], load_sem.at[1]),
    )
    for load in loads:
        load.start()
    barrier = pltpu.get_barrier_semaphore()

    def greet_col(j, carry):
        pl.semaphore_signal(
            barrier, inc=1, device_id=(r, (c + j) % cols), device_id_type=MESH
        )
        return carry

    def greet_row(j, carry):
        pl.semaphore_signal(
            barrier, inc=1, device_id=((r + j) % rows, c), device_id_type=MESH
        )
        return carry

    lax.fori_loop(1, cols, greet_col, 0)
    lax.fori_loop(1, rows, greet_row, 0)
    vals[slots] = jnp.zeros((bs, bs), BF)
    wts[slots] = jnp.zeros((bs, bs), BF)
    wgt[2 * upairs] = jnp.zeros((bs, bs), BF)
    uq_ref[...] = upos_ref[...]
    up_ref[...] = umom_ref[...]
    vq_ref[...] = vpos0_ref[...]
    vp_ref[...] = vmom_ref[...]
    u_own[...] = upos_ref[...].astype(BF).reshape(2, bs, bs)
    v_own[...] = vpos0_ref[...].astype(BF).reshape(2, bs, bs)
    pl.semaphore_wait(barrier, cols + rows - 2)

    def gather_u(j, e):
        return pltpu.make_async_remote_copy(
            src_ref=u_own, dst_ref=u_all.at[e % 2, pl.ds(2 * c, 2)],
            send_sem=agu_s.at[j], recv_sem=agu_r.at[j],
            device_id=(r, (c + j) % cols), device_id_type=MESH,
        )

    def gather_v(j, e):
        return pltpu.make_async_remote_copy(
            src_ref=v_own, dst_ref=v_all.at[pl.ds(2 * r, 2)],
            send_sem=agv_s.at[j], recv_sem=agv_r.at[j],
            device_id=((r + j) % rows, c), device_id_type=MESH,
        )

    def scatter_u(j, e):
        to = (c + j) % cols
        return pltpu.make_async_remote_copy(
            src_ref=u_send.at[pl.ds(2 * to, 2)], dst_ref=u_recv.at[j],
            send_sem=rsu_s.at[j], recv_sem=rsu_r.at[j],
            device_id=(r, to), device_id_type=MESH,
        )

    def scatter_v(j, e):
        to = (r + j) % rows
        return pltpu.make_async_remote_copy(
            src_ref=v_send.at[pl.ds(2 * to, 2)], dst_ref=v_recv.at[j],
            send_sem=rsv_s.at[j], recv_sem=rsv_r.at[j],
            device_id=(to, c), device_id_type=MESH,
        )

    def start(copy, n, e):
        def one(j, carry):
            copy(j, e).start()
            return carry

        lax.fori_loop(1, n, one, 0)

    def wait_recv(copy, n, e):
        def one(j, carry):
            copy(j, e).wait_recv()
            return carry

        lax.fori_loop(1, n, one, 0)

    def wait_send(copy, n, e):
        def one(j, carry):
            copy(j, e).wait_send()
            return carry

        lax.fori_loop(1, n, one, 0)

    start(gather_u, cols, 0)
    start(gather_v, rows, 0)
    u_all[0, pl.ds(2 * c, 2)] = u_own[...]
    v_all[pl.ds(2 * r, 2)] = v_own[...]
    for load in loads:
        load.wait()

    for e in range(LEAPS + 1):
        wait_recv(gather_v, rows, e)
        wait_recv(gather_u, cols, e)

        def first_pass(i, total):
            preds, pairs = [], []
            for g in range(GROUP):
                p = i * GROUP + g
                pair = jnp.concatenate(
                    [v_all[ub_ref[2 * p]], v_all[ub_ref[2 * p + 1]]], axis=0
                )
                pairs.append(pair)
                preds.append(
                    lax.dot_general(
                        u_all[e % 2, ua_ref[p]], pair, NT, preferred_element_type=F32
                    )
                )
            parts = []
            for g in range(GROUP):
                p = i * GROUP + g
                halves = []
                for k in range(2):
                    s = uslot_ref[2 * p + k]
                    resid = vals[s].astype(F32) - preds[g][:, bs * k : bs * (k + 1)]
                    scaled = resid * wts[s].astype(F32)
                    half = scaled * pl.reciprocal(NU_S2 + resid * resid, approx=True)
                    half = half.astype(BF)
                    wgt[2 * p + k] = half
                    halves.append(half)
                parts.append(
                    jnp.dot(
                        jnp.concatenate(halves, axis=1), pairs[g],
                        preferred_element_type=F32,
                    )
                )
            for g in range(GROUP):
                p = i * GROUP + g
                total = jnp.where(ukeep_ref[p] > 0, total, 0.0) + parts[g]
                part[p] = total
            return total

        lax.fori_loop(0, upairs // GROUP, first_pass, jnp.zeros((bs, bs), F32))

        if e > 0:
            wait_send(scatter_u, cols, e)

        def pack_u(a, carry):
            total = part[ulast_ref[a]]
            u_send[a] = jnp.where(usome_ref[a] > 0, total, 0.0).astype(BF)
            return carry

        lax.fori_loop(0, 2 * cols, pack_u, 0)
        start(scatter_u, cols, e)

        def turn(a, carry):
            ut_all[a] = jnp.transpose(u_all[e % 2, a])
            return carry

        lax.fori_loop(0, 2 * cols, turn, 0)

        def second_pass(i, total):
            parts = []
            for g in range(GROUP):
                p = i * GROUP + g
                left = jnp.concatenate(
                    [ut_all[va_ref[2 * p]], ut_all[va_ref[2 * p + 1]]], axis=1
                )
                right = jnp.concatenate(
                    [wgt[vpos_ref[2 * p]], wgt[vpos_ref[2 * p + 1]]], axis=0
                )
                parts.append(jnp.dot(left, right, preferred_element_type=F32))
            for g in range(GROUP):
                p = i * GROUP + g
                total = jnp.where(vkeep_ref[p] > 0, total, 0.0) + parts[g]
                part[p] = total
            return total

        lax.fori_loop(0, vpairs // GROUP, second_pass, jnp.zeros((bs, bs), F32))

        if e > 0:
            wait_send(scatter_v, rows, e)

        def pack_v(b, carry):
            total = part[vlast_ref[b]]
            v_send[b] = jnp.where(vsome_ref[b] > 0, total, 0.0).astype(BF)
            return carry

        lax.fori_loop(0, 2 * rows, pack_v, 0)
        start(scatter_v, rows, e)

        kick = EPS if 0 < e < LEAPS else 0.5 * EPS

        wait_recv(scatter_u, cols, e)
        wait_send(gather_u, cols, e)
        for k in range(2):
            here = pl.ds(bs * k, bs)
            total = u_send[2 * c + k].astype(F32)
            for j in range(1, cols):
                total = total + u_recv[j, k].astype(F32)
            place = uq_ref[here]
            speed = up_ref[here] + kick * (NU1 * total - LAMBDA * place)
            up_ref[here] = speed
            if e < LEAPS:
                place = place + EPS * speed
                uq_ref[here] = place
                u_own[k] = place.astype(BF)
        if e < LEAPS:
            start(gather_u, cols, e + 1)
            u_all[(e + 1) % 2, pl.ds(2 * c, 2)] = u_own[...]

        wait_recv(scatter_v, rows, e)
        wait_send(gather_v, rows, e)
        for k in range(2):
            here = pl.ds(bs * k, bs)
            total = v_send[2 * r + k].astype(F32)
            for j in range(1, rows):
                total = total + v_recv[j, k].astype(F32)
            place = vq_ref[here]
            speed = vp_ref[here] + kick * (NU1 * jnp.transpose(total) - LAMBDA * place)
            vp_ref[here] = speed
            if e < LEAPS:
                place = place + EPS * speed
                vq_ref[here] = place
                v_own[k] = place.astype(BF)
        if e < LEAPS:
            start(gather_v, rows, e + 1)
            v_all[pl.ds(2 * r, 2)] = v_own[...]

    wait_send(scatter_u, cols, LEAPS)
    wait_send(scatter_v, rows, LEAPS)


def body(
    compound_pos, compound_mom, target_pos, target_mom,
    tile_rows, tile_cols, tile_count, tile_values, tile_weight,
):
    cols = lax.axis_size("col")
    rows = lax.axis_size("row")
    slots, bs = tile_values.shape[1], tile_values.shape[2]
    upairs = (slots + 2 * cols) // 2
    vpairs = (slots + 2 * rows) // 2
    row_local = tile_rows[0] - lax.axis_index("row") * (2 * cols)
    holder = tile_cols[0] // 2
    col_local = holder // cols * 2 + tile_cols[0] % 2
    live = jnp.arange(slots, dtype=jnp.int32) < tile_count[0]
    uplace, uat, ua, ukeep, ulast, usome = plan(row_local, live, 2 * cols, upairs)
    uslot = pick(uat, jnp.arange(slots, dtype=jnp.int32), slots)
    ub = pick(uat, col_local, 0)
    _, vat, _, vkeep, vlast, vsome = plan(col_local, live, 2 * rows, vpairs)
    va = pick(vat, row_local, 0)
    vpos = pick(vat, uplace, 2 * upairs)

    smem = pl.BlockSpec(memory_space=pltpu.SMEM)
    vmem = pl.BlockSpec(memory_space=pltpu.VMEM)
    hbm = pl.BlockSpec(memory_space=pl.ANY)
    state = jax.ShapeDtypeStruct(compound_pos.shape, F32)
    sizes = (rows, cols, slots, bs, upairs, vpairs)
    return pl.pallas_call(
        functools.partial(kernel, sizes),
        out_shape=(state,) * 4,
        in_specs=[smem] * 11 + [vmem] * 4 + [hbm] * 2,
        out_specs=(vmem,) * 4,
        scratch_shapes=[
            pltpu.VMEM((slots + 1, bs, bs), BF),
            pltpu.VMEM((slots + 1, bs, bs), BF),
            pltpu.VMEM((2 * upairs + 1, bs, bs), BF),
            pltpu.VMEM((upairs, bs, bs), F32),
            pltpu.VMEM((2, 2 * cols, bs, bs), BF),
            pltpu.VMEM((2 * cols, bs, bs), BF),
            pltpu.VMEM((2 * rows, bs, bs), BF),
            pltpu.VMEM((2, bs, bs), BF),
            pltpu.VMEM((2, bs, bs), BF),
            pltpu.VMEM((2 * cols, bs, bs), BF),
            pltpu.VMEM((cols, 2, bs, bs), BF),
            pltpu.VMEM((2 * rows, bs, bs), BF),
            pltpu.VMEM((rows, 2, bs, bs), BF),
            pltpu.SemaphoreType.DMA((2,)),
            pltpu.SemaphoreType.DMA((cols,)),
            pltpu.SemaphoreType.DMA((cols,)),
            pltpu.SemaphoreType.DMA((rows,)),
            pltpu.SemaphoreType.DMA((rows,)),
            pltpu.SemaphoreType.DMA((cols,)),
            pltpu.SemaphoreType.DMA((cols,)),
            pltpu.SemaphoreType.DMA((rows,)),
            pltpu.SemaphoreType.DMA((rows,)),
        ],
        compiler_params=pltpu.CompilerParams(
            collective_id=0, has_side_effects=True, vmem_limit_bytes=56 << 20
        ),
    )(
        ua, uslot, ub, ukeep, ulast, usome, va, vpos, vkeep, vlast, vsome,
        compound_pos, compound_mom, target_pos, target_mom,
        tile_values[0], tile_weight[0],
    )


def solution(mesh):
    flat = P(("row", "col"), None)
    deep = P(("row", "col"), None, None, None)
    return jax.shard_map(
        body,
        mesh=mesh,
        in_specs=(flat,) * 6 + (P(("row", "col")),) + (deep,) * 2,
        out_specs=(flat,) * 4,
        check_vma=False,
    )
```

time: 1000 us -> 151 us (0.15)
  waiting for transfers between devices: 383 us -> 0 us
  other arithmetic: 251 us -> 9.11 us
  matrix products: 160 us -> 0 us
  Pallas kernels: 0 us -> 133 us
  local copies, waits for them, and re-layouts: 130 us -> 6.27 us
  blocking collectives: 52.1 us -> 0 us
  between operations: 14.6 us -> 1.32 us
    reduce_scatter x6 -> x0, waiting for transfers between devices: 305 us -> none  [the longest x3 218 us: owner_forces(): lax.psum_scatter(comp_acc.astype(jnp.bfloat16), 'col', scatter_dimension=...]
    scatter-add x48 -> x0, other arithmetic: 211 us -> none  [the longest x24 147 us: visit(): comp_acc = carry[0].at[row_ids].add(comp_part)]
    dot_general x72 -> x0, matrix products: 160 us -> none  [the longest x24 61.8 us: tile_terms(): jnp.einsum('tik,tjk->tij', comp_rows, targ_rows, preferred_element_type=j...]
    pallas_call x0 -> x1, Pallas kernels: none -> 133 us  [body(): pl.pallas_call(functools.partial(kernel, sizes), out_shape=(state,) * 4,...]
    gather x48 -> x0, local copies, waits for them, and re-layouts: 99.3 us -> none  [the longest x24 51.9 us: visit(): targ_tiles[col_ids]]
    all_gather x3 -> x0, waiting for transfers between devices: 77.7 us -> none  [owner_forces(): lax.all_gather(comp_now.astype(jnp.bfloat16), 'col', axis=0, tiled=True)]
    all_gather x3 -> x0, blocking collectives: 52.1 us -> none  [owner_forces(): lax.all_gather(targ_now.astype(jnp.bfloat16), 'row', axis=0, tiled=True)]
    convert_element_type x13 -> x2, other arithmetic: 17.3 us -> 1.1 us  [plan(): some = (count > 0).astype(jnp.int32)]
  transfers between devices with their start and end apart: 9 -> 0, of which waited for: 9 -> 0; matrix products, arithmetic and copies ran while one was open for 1% -> 0% of each run, Pallas kernels for 0% -> 0%
where the time goes in v1:
time: 151 us; the launch traced here: 150 us
  Pallas kernels  133 us (88%)
  other arithmetic  9.11 us (6%)
  local copies, waits for them, and re-layouts  6.27 us (4%)
    pallas_call x1, Pallas kernels, body(): pl.pallas_call(functools.partial(kernel, sizes), out_shape=(state,) * 4,...  133 us
    unnamed x4, local copies, waits for them, and re-layouts  6.27 us

profile of v1, /device:TPU:1, one launch (start us, length us, event | category | flops | bytes accessed | tf_op | source)
XLA Modules:
  0.0 149.6 jit_solution(5055060494933550331)
XLA Ops:
  1.3 0.7 broadcast_subtract_fusion
  2.0 0.1 convert_reduce_fusion.2
  2.1 0.5 compare_convert_fusion.1.usome_ref
  2.6 0.1 select_reduce_fusion.7
  2.7 0.6 compare_select_fusion.13
  3.3 0.1 fusion.7
  3.4 0.7 select_reduce_fusion.5.ua_ref
  4.1 0.1 select_reduce_fusion.4
  4.2 0.5 broadcast_select_fusion.5.ukeep_ref
  4.7 0.7 fusion.13
  5.4 0.1 convert_reduce_fusion.3
  5.5 0.6 compare_convert_fusion.vsome_ref
  6.1 0.1 select_reduce_fusion.8
  6.2 0.6 compare_select_fusion.12
  6.8 0.1 fusion.11
  6.9 0.1 select_reduce_fusion.6
  7.0 0.6 broadcast_select_fusion.4.vkeep_ref
  7.6 0.7 fusion.12
  8.3 0.3 convert_reduce_fusion
  8.6 0.2 fusion.1
  8.7 0.2 fusion
  8.9 0.2 select_reduce_fusion.2
  9.0 0.6 broadcast_select_fusion
  9.6 0.2 select_reduce_fusion
  9.8 0.6 broadcast_select_fusion.2
  10.4 132.9 %shard_map.120 = (f32[256,128]{1,0:T(8,128)}, f32[256,128]{1,0:T(8,128)}, f32[256,128]{1,0:T(8,128)}, f32[256,128]{1,0:T(8,128)}) custom-call(s32[144]{0:T(256)} %select_reduce_fusion.5.ua_ref, s32[288]{0:T(512)} %get-tuple-element.17.uslot_ref, s32[288]{0:T(512)} %get-tuple-element.16.ub_ref, s32[144]{0:T(256)} %broadcast_select_fusion.5.ukeep_ref, ...), custom_call_target="tpu_custom_call" | custom-call | tf_op jit(solution)/shard_map/pallas_call | solution.py:316
  143.3 1.6 %copy.18 = f32[256,128]{1,0:T(8,128)} copy(f32[256,128]{1,0:T(8,128)} %get-tuple-element.24) | data formatting | bytes 262144
  144.9 1.6 %copy.19 = f32[256,128]{1,0:T(8,128)} copy(f32[256,128]{1,0:T(8,128)} %get-tuple-element.25) | data formatting | bytes 262144
  146.4 1.6 %copy.20 = f32[256,128]{1,0:T(8,128)} copy(f32[256,128]{1,0:T(8,128)} %get-tuple-element.26) | data formatting | bytes 262144
  148.0 1.6 %copy.21 = f32[256,128]{1,0:T(8,128)} copy(f32[256,128]{1,0:T(8,128)} %get-tuple-element.27) | data formatting | bytes 262144
  (4 shorter events, 0.0 us)

commit v2 on v1

v2 whole, which is shorter than its diff:
```python
import functools

import jax
import jax.numpy as jnp
from jax import lax
from jax.experimental import pallas as pl
from jax.experimental.pallas import tpu as pltpu
from jax.sharding import PartitionSpec as P

MESH = pl.DeviceIdType.MESH
BF = jnp.bfloat16
F32 = jnp.float32
I32 = jnp.int32
NT = (((1,), (1,)), ((), ()))

LEAPS = 2
EPS = 0.01
LAMBDA = 1.0
NU1 = 5.0
NU_S2 = 1.0
SIDE = 4
GROUP1 = 16
GROUP2 = 17
AHEAD = 2
WIDTH = 384
(UA, UKEEP, UB, USLOT, ULAST, USOME, VKEEP, VA, VPOS, VLAST, VSOME) = range(11)


def iota(shape, dim):
    return lax.broadcasted_iota(I32, shape, dim)


def upright(row):
    n = row.shape[1]
    return jnp.sum(
        jnp.where(iota((n, n), 0) == iota((n, n), 1), row, 0), axis=1, keepdims=True
    )


def plan(key, blocks, cap):
    n = key.shape[1]
    col = upright(key)
    before = (key == col) & (iota((n, n), 1) < iota((n, n), 0))
    rank = jnp.sum(jnp.where(before, 1, 0), axis=1, keepdims=True)
    lane = iota((n, 128), 1)
    count = jnp.sum(jnp.where(col == lane, 1, 0), axis=0, keepdims=True)
    count = jnp.where(iota((1, 128), 1) < blocks, count, 0)
    pairs = (count + 1) >> 1
    base = jnp.sum(jnp.where(lane < col, pairs, 0), axis=1, keepdims=True)
    place = jnp.where(col < blocks, 2 * base + rank, 2 * cap)
    count_c = jnp.sum(
        jnp.where(key == iota((blocks, n), 0), 1, 0), axis=1, keepdims=True
    )
    pairs_c = (count_c + 1) >> 1
    b_sub, b_lane = iota((blocks, 128), 0), iota((blocks, 128), 1)
    start_c = jnp.sum(jnp.where(b_lane < b_sub, pairs, 0), axis=1, keepdims=True)
    start = jnp.sum(jnp.where(b_sub < b_lane, pairs_c, 0), axis=0, keepdims=True)
    p = iota((blocks, WIDTH), 1)
    inside = (p >= start_c) & (p < start_c + pairs_c)
    block = jnp.sum(
        jnp.where(inside, iota((blocks, WIDTH), 0), 0), axis=0, keepdims=True
    )
    first = jnp.sum(
        jnp.where(inside & (p == start_c), 1, 0), axis=0, keepdims=True
    )
    last = jnp.where(count > 0, start + pairs - 1, 0)
    some = jnp.where(count > 0, 1, 0)
    hit = place == iota((n, WIDTH), 1)
    return place, hit, block, 1 - first, last, some


def kernel(
    sizes,
    count_ref, trow_ref, tcol_ref, upos_ref, umom_ref, vpos_ref, vmom_ref,
    vals_hbm, wts_hbm,
    uq_ref, up_ref, vq_ref, vp_ref,
    vals, wts, wgt, part, u_all, ut_all, v_all,
    u_send, rs1, mid, rs2, v_send, rv1, vmid, rv2, meta_v, meta,
    load_sem, rs1_s, rs1_r, rs2_s, rs2_r, ag1_s, ag1_r, ag2_s, ag2_r,
    rv1_s, rv1_r, rv2_s, rv2_r, av1_s, av1_r, av2_s, av2_r,
):
    rows, cols, slots, bs, upairs, vpairs = sizes
    r = lax.axis_index("row")
    c = lax.axis_index("col")
    x, y = c // SIDE, c % SIDE
    z, q = r // 2, r % 2

    loads = (
        pltpu.make_async_copy(vals_hbm, vals.at[pl.ds(0, slots)], load_sem.at[0]),
        pltpu.make_async_copy(wts_hbm, wts.at[pl.ds(0, slots)], load_sem.at[1]),
    )
    for load in loads:
        load.start()

    def at(h, s, t):
        return cols * h + SIDE * (s % SIDE) + t % SIDE

    def dev(h, s, t):
        s, t = s % SIDE, t % SIDE
        return (r, SIDE * s + t) if h == 0 else (r, SIDE * t + s)

    st = ((x, y), (y, x))

    def remote(src, dst, send_sem, recv_sem, to):
        return pltpu.make_async_remote_copy(
            src_ref=src, dst_ref=dst, send_sem=send_sem, recv_sem=recv_sem,
            device_id=to, device_id_type=MESH,
        )

    def scatter1(h, m, j):
        s, t = st[h]
        k = SIDE * SIDE * h + SIDE * m + j
        return remote(
            u_send.at[at(h, s + j, t + m)], rs1.at[h, m, j],
            rs1_s.at[k], rs1_r.at[k], dev(h, s + j, t),
        )

    def scatter2(h, m):
        s, t = st[h]
        k = SIDE * h + m
        return remote(
            mid.at[h, m], rs2.at[h, m], rs2_s.at[k], rs2_r.at[k], dev(h, s, t + m)
        )

    def gather1(h, m, par):
        s, t = st[h]
        k = SIDE * h + m
        ref = u_all.at[par, at(h, s, t)]
        return remote(ref, ref, ag1_s.at[k], ag1_r.at[k], dev(h, s, t + m))

    def gather2(h, m, j, par):
        s, t = st[h]
        k = SIDE * SIDE * h + SIDE * m + j
        ref = u_all.at[par, at(h, s, t + SIDE - m)]
        return remote(ref, ref, ag2_s.at[k], ag2_r.at[k], dev(h, s + j, t))

    def vspan(core, zz):
        return pl.ds(rows * core + 2 * (zz % SIDE), 2)

    sibling = (2 * z + 1 - q, c)

    def zdev(m):
        return (2 * ((z + m) % SIDE) + q, c)

    def vscatter1(m):
        return remote(
            v_send.at[vspan(1 - q, z + m)], rv1.at[m], rv1_s.at[m], rv1_r.at[m], sibling
        )

    def vscatter2(m):
        return remote(vmid.at[m], rv2.at[m], rv2_s.at[m], rv2_r.at[m], zdev(m))

    def vgather1(m):
        ref = v_all.at[vspan(q, z)]
        return remote(ref, ref, av1_s.at[m], av1_r.at[m], zdev(m))

    def vgather2(m):
        ref = v_all.at[vspan(q, z + SIDE - m)]
        return remote(ref, ref, av2_s.at[m], av2_r.at[m], sibling)

    def each(act, *bounds):
        def nest(done, left):
            if not left:
                act(*done)
                return

            def step(i, carry):
                nest(done + (i,), left[1:])
                return carry

            lax.fori_loop(left[0][0], left[0][1], step, 0)

        nest((), bounds)

    others = (1, SIDE)
    everyone = (0, SIDE)

    def start_gather(par):
        for h in range(2):
            each(lambda m: gather1(h, m, par).start(), others)
        for h in range(2):
            each(lambda j: gather2(h, 0, j, par).start(), others)

    def forward_gather(par):
        def pass_on(m):
            for h in range(2):
                gather1(h, m, par).wait_recv()
                each(lambda j: gather2(h, m, j, par).start(), others)

        each(pass_on, others)

    def finish_gather(par):
        for h in range(2):
            each(lambda m, j: gather2(h, m, j, par).wait_recv(), everyone, others)

    def clear_gather(par):
        for h in range(2):
            each(lambda m: gather1(h, m, par).wait_send(), others)
            each(lambda m, j: gather2(h, m, j, par).wait_send(), everyone, others)

    def start_vgather():
        each(lambda m: vgather1(m).start(), others)
        vgather2(0).start()

    def forward_vgather():
        def pass_on(m):
            vgather1(m).wait_recv()
            vgather2(m).start()

        each(pass_on, others)

    def finish_vgather():
        each(lambda m: vgather2(m).wait_recv(), everyone)

    def clear_vgather():
        each(lambda m: vgather1(m).wait_send(), others)
        each(lambda m: vgather2(m).wait_send(), everyone)

    barrier = pltpu.get_barrier_semaphore()

    def greet(to):
        pl.semaphore_signal(barrier, inc=1, device_id=to, device_id_type=MESH)

    each(lambda m: greet(dev(0, x + m, y)), others)
    each(lambda m: greet(dev(0, x, y + m)), others)
    each(lambda m: greet(zdev(m)), others)
    greet(sibling)
    for h in range(2):
        here = pl.ds(bs * h, bs)
        u_all[0, at(h, *st[h])] = upos_ref[here].astype(BF)
        v_all[rows * q + 2 * z + h] = vpos_ref[here].astype(BF)
    pl.semaphore_wait(barrier, 3 * (SIDE - 1) + 1)
    start_gather(0)
    start_vgather()

    vals[slots] = jnp.zeros((bs, bs), BF)
    wts[slots] = jnp.zeros((bs, bs), BF)
    wgt[2 * upairs] = jnp.zeros((bs, bs), BF)
    uq_ref[...] = upos_ref[...]
    up_ref[...] = umom_ref[...]
    vq_ref[...] = vpos_ref[...]
    vp_ref[...] = vmom_ref[...]

    live = iota((1, slots), 1) < count_ref[0]
    block = trow_ref[...] - r * (2 * cols)
    owner = block >> 1
    ukey = jnp.where(
        block % 2 == 0, owner, cols + SIDE * (owner % SIDE) + owner // SIDE
    )
    owner = tcol_ref[...] // (2 * cols)
    vkey = rows * (owner % 2) + 2 * (owner // 2) + tcol_ref[...] % 2
    uid, vid = upright(ukey), upright(vkey)
    ukey = jnp.where(live, ukey, 127)
    vkey = jnp.where(live, vkey, 127)

    meta_v[...] = jnp.zeros(meta_v.shape, I32)

    def put(k, row):
        meta_v[pl.ds(k, 1), pl.ds(0, row.shape[1])] = row

    def chosen(hit, values, default):
        return (
            jnp.sum(jnp.where(hit, values - default, 0), axis=0, keepdims=True)
            + default
        )

    place, hit, block, keep, last, some = plan(ukey, 2 * cols, upairs)
    put(UA, block)
    put(UKEEP, keep)
    put(ULAST, last)
    put(USOME, some)
    put(UB, chosen(hit, vid, 0))
    put(USLOT, chosen(hit, iota((slots, 1), 0), slots))
    _, hit, _, keep, last, some = plan(vkey, 2 * rows, vpairs)
    put(VKEEP, keep)
    put(VLAST, last)
    put(VSOME, some)
    put(VA, chosen(hit, uid, 0))
    put(VPOS, chosen(hit, place, 2 * upairs))
    to_smem = pltpu.make_async_copy(meta_v, meta, load_sem.at[2])
    to_smem.start()

    forward_vgather()
    forward_gather(0)
    to_smem.wait()
    for load in loads:
        load.wait()

    for e in range(LEAPS + 1):
        par = e % 2
        finish_vgather()
        finish_gather(par)

        def first_pass(i, total):
            preds, pairs, halves = {}, {}, {}
            for g in range(GROUP1 + AHEAD + 1):
                if g < GROUP1:
                    p = i * GROUP1 + g
                    pairs[g] = jnp.concatenate(
                        [v_all[meta[UB, 2 * p]], v_all[meta[UB, 2 * p + 1]]], axis=0
                    )
                    preds[g] = lax.dot_general(
                        u_all[par, meta[UA, p]], pairs[g], NT, preferred_element_type=F32
                    )
                b = g - AHEAD
                if 0 <= b < GROUP1:
                    for k in range(2):
                        at_slot = 2 * (i * GROUP1 + b) + k
                        s = meta[USLOT, at_slot]
                        resid = vals[s].astype(F32) - preds[b][:, bs * k : bs * (k + 1)]
                        resid = resid.astype(BF)
                        inverse = pl.reciprocal(BF(NU_S2) + resid * resid, approx=True)
                        half = (resid * wts[s]) * inverse
                        wgt[at_slot] = half
                        halves[b, k] = half
                b = b - 1
                if 0 <= b < GROUP1:
                    p = i * GROUP1 + b
                    term = jnp.dot(
                        jnp.concatenate([halves[b, 0], halves[b, 1]], axis=1),
                        pairs[b], preferred_element_type=F32,
                    )
                    total = jnp.where(meta[UKEEP, p] > 0, total, 0.0) + term
                    part[p] = total
            return total

        lax.fori_loop(0, upairs // GROUP1, first_pass, jnp.zeros((bs, bs), F32))

        clear_gather(par)
        clear_vgather()
        if e > 0:
            for h in range(2):
                each(lambda m, j: scatter1(h, m, j).wait_send(), everyone, others)

        def pack_u(a, carry):
            total = part[meta[ULAST, a]]
            u_send[a] = jnp.where(meta[USOME, a] > 0, total, 0.0).astype(BF)
            return carry

        lax.fori_loop(0, 2 * cols, pack_u, 0)
        for h in range(2):
            each(lambda m, j: scatter1(h, m, j).start(), others, others)
        for h in range(2):
            each(lambda j: scatter1(h, 0, j).start(), others)

        def turn(a, carry):
            ut_all[a] = jnp.transpose(u_all[par, a])
            return carry

        lax.fori_loop(0, 2 * cols, turn, 0)

        def second_pass(i, total):
            for g in range(GROUP2):
                p = i * GROUP2 + g
                left = jnp.concatenate(
                    [ut_all[meta[VA, 2 * p]], ut_all[meta[VA, 2 * p + 1]]], axis=1
                )
                right = jnp.concatenate(
                    [wgt[meta[VPOS, 2 * p]], wgt[meta[VPOS, 2 * p + 1]]], axis=0
                )
                term = jnp.dot(left, right, preferred_element_type=F32)
                total = jnp.where(meta[VKEEP, p] > 0, total, 0.0) + term
                part[p] = total
            return total

        lax.fori_loop(0, vpairs // GROUP2, second_pass, jnp.zeros((bs, bs), F32))

        if e > 0:
            each(lambda m: vscatter1(m).wait_send(), everyone)

        def pack_v(b, carry):
            total = part[meta[VLAST, b]]
            v_send[b] = jnp.where(meta[VSOME, b] > 0, total, 0.0).astype(BF)
            return carry

        lax.fori_loop(0, 2 * rows, pack_v, 0)
        each(lambda m: vscatter1(m).start(), others)
        vscatter1(0).start()

        if e > 0:
            for h in range(2):
                each(lambda m: scatter2(h, m).wait_send(), others)
            each(lambda m: vscatter2(m).wait_send(), others)

        def sum1(h, m):
            each(lambda j: scatter1(h, m, j).wait_recv(), others)
            s, t = st[h]
            total = u_send[at(h, s, t + m)].astype(F32)
            for j in range(1, SIDE):
                total = total + rs1[h, m, j].astype(F32)
            return total

        def relay(m):
            for h in range(2):
                mid[h, m] = sum1(h, m).astype(BF)
                scatter2(h, m).start()

        each(relay, others)

        def vrelay(m):
            vscatter1(m).wait_recv()
            total = v_send[vspan(q, z + m)].astype(F32) + rv1[m].astype(F32)
            vmid[m] = total.astype(BF)
            vscatter2(m).start()

        each(vrelay, others)

        kick = EPS if 0 < e < LEAPS else 0.5 * EPS

        def advance(q_ref, p_ref, k, total):
            here = pl.ds(bs * k, bs)
            place = q_ref[here]
            speed = p_ref[here] + kick * (NU1 * total - LAMBDA * place)
            p_ref[here] = speed
            if e < LEAPS:
                place = place + EPS * speed
                q_ref[here] = place
            return place

        for h in range(2):
            total = sum1(h, 0)
            for m in range(1, SIDE):
                scatter2(h, m).wait_recv()
                total = total + rs2[h, m].astype(F32)
            place = advance(uq_ref, up_ref, h, total)
            if e < LEAPS:
                u_all[1 - par, at(h, *st[h])] = place.astype(BF)
        if e < LEAPS:
            start_gather(1 - par)

        vscatter1(0).wait_recv()
        each(lambda m: vscatter2(m).wait_recv(), others)
        for k in range(2):
            b = rows * q + 2 * z + k
            total = v_send[b].astype(F32) + rv1[0, k].astype(F32)
            for m in range(1, SIDE):
                total = total + rv2[m, k].astype(F32)
            place = advance(vq_ref, vp_ref, k, jnp.transpose(total))
            if e < LEAPS:
                v_all[b] = place.astype(BF)
        if e < LEAPS:
            start_vgather()
            forward_gather(1 - par)
            forward_vgather()

    for h in range(2):
        each(lambda m, j: scatter1(h, m, j).wait_send(), everyone, others)
        each(lambda m: scatter2(h, m).wait_send(), others)
    each(lambda m: vscatter1(m).wait_send(), everyone)
    each(lambda m: vscatter2(m).wait_send(), others)


def settle(*refs):
    ins, outs, sem = refs[:4], refs[4:8], refs[8]
    copies = [
        pltpu.make_async_copy(a, b, sem.at[k]) for k, (a, b) in enumerate(zip(ins, outs))
    ]
    for copy in copies:
        copy.start()
    for copy in copies:
        copy.wait()


def body(
    compound_pos, compound_mom, target_pos, target_mom,
    tile_rows, tile_cols, tile_count, tile_values, tile_weight,
):
    cols = lax.axis_size("col")
    rows = lax.axis_size("row")
    slots, bs = tile_values.shape[1], tile_values.shape[2]
    upairs = (slots + 2 * cols) // 2
    vpairs = (slots + 2 * rows) // 2
    smem = pl.BlockSpec(memory_space=pltpu.SMEM)
    vmem = pl.BlockSpec(memory_space=pltpu.VMEM)
    hbm = pl.BlockSpec(memory_space=pl.ANY)
    state = jax.ShapeDtypeStruct(compound_pos.shape, F32)
    sizes = (rows, cols, slots, bs, upairs, vpairs)
    dma = pltpu.SemaphoreType.DMA
    full, step = 2 * SIDE * SIDE, 2 * SIDE
    out = pl.pallas_call(
        functools.partial(kernel, sizes),
        out_shape=(state,) * 4,
        in_specs=[smem] + [vmem] * 6 + [hbm] * 2,
        out_specs=(vmem,) * 4,
        scratch_shapes=[
            pltpu.VMEM((slots + 1, bs, bs), BF),
            pltpu.VMEM((slots + 1, bs, bs), BF),
            pltpu.VMEM((2 * upairs + 1, bs, bs), BF),
            pltpu.VMEM((upairs, bs, bs), F32),
            pltpu.VMEM((2, 2 * cols, bs, bs), BF),
            pltpu.VMEM((2 * cols, bs, bs), BF),
            pltpu.VMEM((2 * rows, bs, bs), BF),
            pltpu.VMEM((2 * cols, bs, bs), BF),
            pltpu.VMEM((2, SIDE, SIDE, bs, bs), BF),
            pltpu.VMEM((2, SIDE, bs, bs), BF),
            pltpu.VMEM((2, SIDE, bs, bs), BF),
            pltpu.VMEM((2 * rows, bs, bs), BF),
            pltpu.VMEM((SIDE, 2, bs, bs), BF),
            pltpu.VMEM((SIDE, 2, bs, bs), BF),
            pltpu.VMEM((SIDE, 2, bs, bs), BF),
            pltpu.VMEM((16, WIDTH), I32),
            pltpu.SMEM((16, WIDTH), I32),
            dma((3,)),
            dma((full,)), dma((full,)), dma((step,)), dma((step,)),
            dma((step,)), dma((step,)), dma((full,)), dma((full,)),
            dma((SIDE,)), dma((SIDE,)), dma((SIDE,)), dma((SIDE,)),
            dma((SIDE,)), dma((SIDE,)), dma((SIDE,)), dma((SIDE,)),
        ],
        compiler_params=pltpu.CompilerParams(
            collective_id=0, has_side_effects=True, vmem_limit_bytes=56 << 20
        ),
    )(
        tile_count, tile_rows, tile_cols, compound_pos, compound_mom,
        target_pos, target_mom, tile_values[0], tile_weight[0],
    )
    return pl.pallas_call(
        settle,
        out_shape=(state,) * 4,
        in_specs=[hbm] * 4,
        out_specs=(hbm,) * 4,
        scratch_shapes=[dma((4,))],
    )(*out)


def solution(mesh):
    flat = P(("row", "col"), None)
    deep = P(("row", "col"), None, None, None)
    return jax.shard_map(
        body,
        mesh=mesh,
        in_specs=(flat,) * 6 + (P(("row", "col")),) + (deep,) * 2,
        out_specs=(flat,) * 4,
        check_vma=False,
    )
```

time: 151 us -> 119 us (0.79); the launches traced: 150 us -> 119 us
  Pallas kernels: 133 us -> 118 us
  other arithmetic: 9.11 us -> 0 us
  local copies, waits for them, and re-layouts: 6.27 us -> 0 us
    pallas_call x1, Pallas kernels: 133 us -> 101 us  [body(): pl.pallas_call(functools.partial(kernel, sizes), out_shape=(state,) * 4,...]
    pallas_call x0 -> x1, Pallas kernels: none -> 17 us  [body(): pl.pallas_call(settle, out_shape=(state,) * 4, in_specs=[hbm] * 4, out_sp...]
    unnamed x4 -> x0, local copies, waits for them, and re-layouts: 6.27 us -> none
    select_n x9 -> x0, other arithmetic: 3.49 us -> none  [the longest x2 1.18 us: pick(): return jnp.where(hit, got, default).astype(jnp.int32)]
    reduce_sum x10 -> x0, other arithmetic: 1.95 us -> none  [the longest x1 0.68 us: plan(): block = (inside * ids[None, :]).sum(1).astype(jnp.int32)]
where the time goes in v2:
time: 119 us
  Pallas kernels  118 us (99%)
  between operations  1.29 us (1%)
    pallas_call x1, Pallas kernels, body(): pl.pallas_call(functools.partial(kernel, sizes), out_shape=(state,) * 4,...  101 us
    pallas_call x1, Pallas kernels, body(): pl.pallas_call(settle, out_shape=(state,) * 4, in_specs=[hbm] * 4, out_sp...  17 us

profile of v2, /device:TPU:1, one launch (start us, length us, event | category | flops | bytes accessed | tf_op | source)
XLA Modules:
  0.0 119.2 jit_solution(1162316207130570044)
XLA Ops:
  1.3 100.8 %shard_map.120 = (f32[256,128]{1,0:T(8,128)}, f32[256,128]{1,0:T(8,128)}, f32[256,128]{1,0:T(8,128)}, f32[256,128]{1,0:T(8,128)}) custom-call(s32[1]{0:T(128)S(6)} %copy.13.count_ref, s32[1,256]{1,0:T(1,128)} %trow_ref.1, s32[1,256]{1,0:T(1,128)} %tcol_ref.1, f32[256,128]{1,0:T(8,128)} %upos_ref.1, f32[256,128]{1,0:T(8,128)} %umom_ref.1, ...), custom_call_target="tpu_custom_call" | custom-call | tf_op jit(solution)/shard_map/pallas_call | solution.py:480
  102.1 17.0 %shard_map.121 = (f32[256,128]{1,0:T(8,128)}, f32[256,128]{1,0:T(8,128)}, f32[256,128]{1,0:T(8,128)}, f32[256,128]{1,0:T(8,128)}) custom-call(f32[256,128]{1,0:T(8,128)} %get-tuple-element.8.refs_0_, f32[256,128]{1,0:T(8,128)} %get-tuple-element.9.refs_1_, f32[256,128]{1,0:T(8,128)} %get-tuple-element.10.refs_2_, f32[256,128]{1,0:T(8,128)} %get-tuple-element.11.refs_3_), custom_call_target="tpu_custom_call" | custom-call | tf_op jit(solution)/shard_map/pallas_call | solution.py:516

commit v3 on v2

--- a/solution.py
+++ b/solution.py
@@ -19,7 +19,7 @@
 NU1 = 5.0
 NU_S2 = 1.0
 SIDE = 4
-GROUP1 = 16
+GROUP1 = 24
 GROUP2 = 17
 AHEAD = 2
 WIDTH = 384
@@ -73,7 +73,7 @@
     sizes,
     count_ref, trow_ref, tcol_ref, upos_ref, umom_ref, vpos_ref, vmom_ref,
     vals_hbm, wts_hbm,
-    uq_ref, up_ref, vq_ref, vp_ref,
+    uq_ref, up_ref, ut_ref, vq_ref, vp_ref, vt_ref,
     vals, wts, wgt, part, u_all, ut_all, v_all,
     u_send, rs1, mid, rs2, v_send, rv1, vmid, rv2, meta_v, meta,
     load_sem, rs1_s, rs1_r, rs2_s, rs2_r, ag1_s, ag1_r, ag2_s, ag2_r,
@@ -163,12 +163,8 @@
             if not left:
                 act(*done)
                 return
-
-            def step(i, carry):
-                nest(done + (i,), left[1:])
-                return carry
-
-            lax.fori_loop(left[0][0], left[0][1], step, 0)
+            for k in range(*left[0]):
+                nest(done + (k,), left[1:])
 
         nest((), bounds)
 
@@ -326,12 +322,6 @@
 
         lax.fori_loop(0, upairs // GROUP1, first_pass, jnp.zeros((bs, bs), F32))
 
-        clear_gather(par)
-        clear_vgather()
-        if e > 0:
-            for h in range(2):
-                each(lambda m, j: scatter1(h, m, j).wait_send(), everyone, others)
-
         def pack_u(a, carry):
             total = part[meta[ULAST, a]]
             u_send[a] = jnp.where(meta[USOME, a] > 0, total, 0.0).astype(BF)
@@ -342,6 +332,8 @@
             each(lambda m, j: scatter1(h, m, j).start(), others, others)
         for h in range(2):
             each(lambda j: scatter1(h, 0, j).start(), others)
+
+        clear_vgather()
 
         def turn(a, carry):
             ut_all[a] = jnp.transpose(u_all[par, a])
@@ -365,9 +357,6 @@
 
         lax.fori_loop(0, vpairs // GROUP2, second_pass, jnp.zeros((bs, bs), F32))
 
-        if e > 0:
-            each(lambda m: vscatter1(m).wait_send(), everyone)
-
         def pack_v(b, carry):
             total = part[meta[VLAST, b]]
             v_send[b] = jnp.where(meta[VSOME, b] > 0, total, 0.0).astype(BF)
@@ -377,10 +366,7 @@
         each(lambda m: vscatter1(m).start(), others)
         vscatter1(0).start()
 
-        if e > 0:
-            for h in range(2):
-                each(lambda m: scatter2(h, m).wait_send(), others)
-            each(lambda m: vscatter2(m).wait_send(), others)
+        clear_gather(par)
 
         def sum1(h, m):
             each(lambda j: scatter1(h, m, j).wait_recv(), others)
@@ -407,22 +393,25 @@
 
         kick = EPS if 0 < e < LEAPS else 0.5 * EPS
 
-        def advance(q_ref, p_ref, k, total):
+        def advance(q_ref, p_ref, total_ref, k, total):
             here = pl.ds(bs * k, bs)
+            if e == LEAPS:
+                total_ref[here] = total
+                return None
             place = q_ref[here]
+            if e > 0:
+                place = place + EPS * p_ref[here]
+                q_ref[here] = place
             speed = p_ref[here] + kick * (NU1 * total - LAMBDA * place)
             p_ref[here] = speed
-            if e < LEAPS:
-                place = place + EPS * speed
-                q_ref[here] = place
-            return place
+            return place + EPS * speed
 
         for h in range(2):
             total = sum1(h, 0)
             for m in range(1, SIDE):
                 scatter2(h, m).wait_recv()
                 total = total + rs2[h, m].astype(F32)
-            place = advance(uq_ref, up_ref, h, total)
+            place = advance(uq_ref, up_ref, ut_ref, h, total)
             if e < LEAPS:
                 u_all[1 - par, at(h, *st[h])] = place.astype(BF)
         if e < LEAPS:
@@ -435,30 +424,18 @@
             total = v_send[b].astype(F32) + rv1[0, k].astype(F32)
             for m in range(1, SIDE):
                 total = total + rv2[m, k].astype(F32)
-            place = advance(vq_ref, vp_ref, k, jnp.transpose(total))
+            place = advance(vq_ref, vp_ref, vt_ref, k, jnp.transpose(total))
             if e < LEAPS:
                 v_all[b] = place.astype(BF)
         if e < LEAPS:
             start_vgather()
             forward_gather(1 - par)
             forward_vgather()
-
-    for h in range(2):
-        each(lambda m, j: scatter1(h, m, j).wait_send(), everyone, others)
-        each(lambda m: scatter2(h, m).wait_send(), others)
-    each(lambda m: vscatter1(m).wait_send(), everyone)
-    each(lambda m: vscatter2(m).wait_send(), others)
-
-
-def settle(*refs):
-    ins, outs, sem = refs[:4], refs[4:8], refs[8]
-    copies = [
-        pltpu.make_async_copy(a, b, sem.at[k]) for k, (a, b) in enumerate(zip(ins, outs))
-    ]
-    for copy in copies:
-        copy.start()
-    for copy in copies:
-        copy.wait()
+        for h in range(2):
+            each(lambda m, j: scatter1(h, m, j).wait_send(), everyone, others)
+            each(lambda m: scatter2(h, m).wait_send(), others)
+        each(lambda m: vscatter1(m).wait_send(), everyone)
+        each(lambda m: vscatter2(m).wait_send(), others)
 
 
 def body(
@@ -479,9 +456,9 @@
     full, step = 2 * SIDE * SIDE, 2 * SIDE
     out = pl.pallas_call(
         functools.partial(kernel, sizes),
-        out_shape=(state,) * 4,
+        out_shape=(state,) * 6,
         in_specs=[smem] + [vmem] * 6 + [hbm] * 2,
-        out_specs=(vmem,) * 4,
+        out_specs=(vmem,) * 6,
         scratch_shapes=[
             pltpu.VMEM((slots + 1, bs, bs), BF),
             pltpu.VMEM((slots + 1, bs, bs), BF),
@@ -513,13 +490,11 @@
         tile_count, tile_rows, tile_cols, compound_pos, compound_mom,
         target_pos, target_mom, tile_values[0], tile_weight[0],
     )
-    return pl.pallas_call(
-        settle,
-        out_shape=(state,) * 4,
-        in_specs=[hbm] * 4,
-        out_specs=(hbm,) * 4,
-        scratch_shapes=[dma((4,))],
-    )(*out)
+    ends = []
+    for place, speed, total in (out[:3], out[3:]):
+        place = place + EPS * speed
+        ends += [place, speed + 0.5 * EPS * (NU1 * total - LAMBDA * place)]
+    return tuple(ends)
 
 
 def solution(mesh):

time: 119 us -> 98.9 us (0.83)
  Pallas kernels: 118 us -> 95.4 us
  other arithmetic: 0 us -> 2.03 us
    pallas_call x2 -> x1, Pallas kernels: 118 us -> 95.4 us  [body(): pl.pallas_call(functools.partial(kernel, sizes), out_shape=(state,) * 6,...]
    add x0 -> x1, other arithmetic: none -> 2.03 us  [body(): ends += [place, speed + 0.5 * EPS * (NU1 * total - LAMBDA * place)]]
where the time goes in v3:
time: 98.9 us; the launch traced here: 98.7 us
  Pallas kernels  95.4 us (96%)
  other arithmetic  2.03 us (2%)
  between operations  1.29 us (1%)
    pallas_call x1, Pallas kernels, body(): pl.pallas_call(functools.partial(kernel, sizes), out_shape=(state,) * 6,...  95.4 us
    add x1, other arithmetic, body(): ends += [place, speed + 0.5 * EPS * (NU1 * total - LAMBDA * place)]  2.03 us

profile of v3, /device:TPU:1, one launch (start us, length us, event | category | flops | bytes accessed | tf_op | source)
XLA Modules:
  0.0 98.7 jit_solution(10982484404033750747)
XLA Ops:
  1.3 95.4 %shard_map.120 = (f32[256,128]{1,0:T(8,128)}, f32[256,128]{1,0:T(8,128)}, f32[256,128]{1,0:T(8,128)}, f32[256,128]{1,0:T(8,128)}, f32[256,128]{1,0:T(8,128)}, /*index=5*/f32[256,128]{1,0:T(8,128)}) custom-call(s32[1]{0:T(128)S(6)} %copy.13.count_ref, s32[1,256]{1,0:T(1,128)} %trow_ref.1, s32[1,256]{1,0:T(1,128)} %tcol_ref.1, f32[256,128]{1,0:T(8,128)} %upos_ref.1, ...), custom_call_target="tpu_custom_call" | custom-call | tf_op jit(solution)/shard_map/pallas_call | solution.py:457
  96.7 2.0 %multiply_add_fusion = (f32[256,128]{1,0:T(8,128)}, f32[256,128]{1,0:T(8,128)}, f32[256,128]{1,0:T(8,128)}, f32[256,128]{1,0:T(8,128)}) fusion(f32[256,128]{1,0:T(8,128)} %get-tuple-element.14, f32[256,128]{1,0:T(8,128)} %get-tuple-element.15, f32[256,128]{1,0:T(8,128)} %get-tuple-element.13, f32[256,128]{1,0:T(8,128)} %get-tuple-element.11, ...), kind=kLoop, calls=%fused_computation | loop fusion | flops 393216 | bytes 1310720 | tf_op jit(solution)/shard_map/add | solution.py:496

commit v4 on v3

--- a/solution.py
+++ b/solution.py
@@ -19,7 +19,7 @@
 NU1 = 5.0
 NU_S2 = 1.0
 SIDE = 4
-GROUP1 = 24
+GROUP1 = 36
 GROUP2 = 17
 AHEAD = 2
 WIDTH = 384
@@ -71,8 +71,10 @@
 
 def kernel(
     sizes,
-    count_ref, trow_ref, tcol_ref, upos_ref, umom_ref, vpos_ref, vmom_ref,
+    count_hbm, trow_hbm, tcol_hbm, upos_hbm, umom_hbm, vpos_hbm, vmom_hbm,
     vals_hbm, wts_hbm,
+    uq_out, up_out, ut_out, vq_out, vp_out, vt_out,
+    count_ref, trow_ref, tcol_ref,
     uq_ref, up_ref, ut_ref, vq_ref, vp_ref, vt_ref,
     vals, wts, wgt, part, u_all, ut_all, v_all,
     u_send, rs1, mid, rs2, v_send, rv1, vmid, rv2, meta_v, meta,
@@ -85,12 +87,13 @@
     x, y = c // SIDE, c % SIDE
     z, q = r // 2, r % 2
 
-    loads = (
-        pltpu.make_async_copy(vals_hbm, vals.at[pl.ds(0, slots)], load_sem.at[0]),
-        pltpu.make_async_copy(wts_hbm, wts.at[pl.ds(0, slots)], load_sem.at[1]),
-    )
-    for load in loads:
-        load.start()
+    def load(src, dst, k):
+        copy = pltpu.make_async_copy(src, dst, load_sem.at[k])
+        copy.start()
+        return copy
+
+    load_u = load(upos_hbm, uq_ref, 3)
+    load_v = load(vpos_hbm, vq_ref, 4)
 
     def at(h, s, t):
         return cols * h + SIDE * (s % SIDE) + t % SIDE
@@ -163,19 +166,20 @@
             if not left:
                 act(*done)
                 return
-            for k in range(*left[0]):
+            for k in left[0]:
                 nest(done + (k,), left[1:])
 
         nest((), bounds)
 
-    others = (1, SIDE)
-    everyone = (0, SIDE)
-
-    def start_gather(par):
-        for h in range(2):
-            each(lambda m: gather1(h, m, par).start(), others)
-        for h in range(2):
-            each(lambda j: gather2(h, 0, j, par).start(), others)
+    others = (2, 1, 3)
+    everyone = (0, 2, 1, 3)
+
+    def start_gather(h, par):
+        each(lambda m: gather1(h, m, par).start(), others)
+        each(lambda j: gather2(h, 0, j, par).start(), others)
+
+    def turn(a, par):
+        ut_all[a] = jnp.transpose(u_all[par, a])
 
     def forward_gather(par):
         def pass_on(m):
@@ -187,7 +191,16 @@
 
     def finish_gather(par):
         for h in range(2):
-            each(lambda m, j: gather2(h, m, j, par).wait_recv(), everyone, others)
+            s, t = st[h]
+            each(lambda m: turn(at(h, s, t + m), par), everyone)
+
+        def take(m, j):
+            for h in range(2):
+                s, t = st[h]
+                gather2(h, m, j, par).wait_recv()
+                turn(at(h, s + SIDE - j, t + SIDE - m), par)
+
+        each(take, everyone, others)
 
     def clear_gather(par):
         for h in range(2):
@@ -221,21 +234,32 @@
     each(lambda m: greet(dev(0, x, y + m)), others)
     each(lambda m: greet(zdev(m)), others)
     greet(sibling)
+    load_lists = (
+        load(count_hbm, count_ref, 5),
+        load(trow_hbm, trow_ref, 6),
+        load(tcol_hbm, tcol_ref, 7),
+    )
+    load_speeds = (load(umom_hbm, up_ref, 8), load(vmom_hbm, vp_ref, 9))
+    loads = (
+        load(vals_hbm, vals.at[pl.ds(0, slots)], 0),
+        load(wts_hbm, wts.at[pl.ds(0, slots)], 1),
+    )
+    load_u.wait()
+    load_v.wait()
     for h in range(2):
         here = pl.ds(bs * h, bs)
-        u_all[0, at(h, *st[h])] = upos_ref[here].astype(BF)
-        v_all[rows * q + 2 * z + h] = vpos_ref[here].astype(BF)
+        u_all[0, at(h, *st[h])] = uq_ref[here].astype(BF)
+        v_all[rows * q + 2 * z + h] = vq_ref[here].astype(BF)
     pl.semaphore_wait(barrier, 3 * (SIDE - 1) + 1)
-    start_gather(0)
+    start_gather(0, 0)
+    start_gather(1, 0)
     start_vgather()
 
     vals[slots] = jnp.zeros((bs, bs), BF)
     wts[slots] = jnp.zeros((bs, bs), BF)
     wgt[2 * upairs] = jnp.zeros((bs, bs), BF)
-    uq_ref[...] = upos_ref[...]
-    up_ref[...] = umom_ref[...]
-    vq_ref[...] = vpos_ref[...]
-    vp_ref[...] = vmom_ref[...]
+    for copy in load_lists:
+        copy.wait()
 
     live = iota((1, slots), 1) < count_ref[0]
     block = trow_ref[...] - r * (2 * cols)
@@ -279,8 +303,8 @@
     forward_vgather()
     forward_gather(0)
     to_smem.wait()
-    for load in loads:
-        load.wait()
+    for copy in (*loads, *load_speeds):
+        copy.wait()
 
     for e in range(LEAPS + 1):
         par = e % 2
@@ -322,24 +346,23 @@
 
         lax.fori_loop(0, upairs // GROUP1, first_pass, jnp.zeros((bs, bs), F32))
 
-        def pack_u(a, carry):
+        def pack_u(a):
             total = part[meta[ULAST, a]]
             u_send[a] = jnp.where(meta[USOME, a] > 0, total, 0.0).astype(BF)
-            return carry
-
-        lax.fori_loop(0, 2 * cols, pack_u, 0)
+
+        def send(m, j):
+            for h in range(2):
+                s, t = st[h]
+                pack_u(at(h, s + j, t + m))
+                scatter1(h, m, j).start()
+
+        each(send, others, others)
+        each(lambda j: send(0, j), others)
         for h in range(2):
-            each(lambda m, j: scatter1(h, m, j).start(), others, others)
-        for h in range(2):
-            each(lambda j: scatter1(h, 0, j).start(), others)
+            s, t = st[h]
+            each(lambda m: pack_u(at(h, s, t + m)), everyone)
 
         clear_vgather()
-
-        def turn(a, carry):
-            ut_all[a] = jnp.transpose(u_all[par, a])
-            return carry
-
-        lax.fori_loop(0, 2 * cols, turn, 0)
 
         def second_pass(i, total):
             for g in range(GROUP2):
@@ -381,7 +404,6 @@
                 mid[h, m] = sum1(h, m).astype(BF)
                 scatter2(h, m).start()
 
-        each(relay, others)
 
         def vrelay(m):
             vscatter1(m).wait_recv()
@@ -389,9 +411,17 @@
             vmid[m] = total.astype(BF)
             vscatter2(m).start()
 
+        relay(1)
         each(vrelay, others)
+        relay(2)
+        relay(3)
 
         kick = EPS if 0 < e < LEAPS else 0.5 * EPS
+        if e == LEAPS:
+            stores = [
+                load(uq_ref, uq_out, 3), load(up_ref, up_out, 4),
+                load(vq_ref, vq_out, 5), load(vp_ref, vp_out, 6),
+            ]
 
         def advance(q_ref, p_ref, total_ref, k, total):
             here = pl.ds(bs * k, bs)
@@ -414,8 +444,10 @@
             place = advance(uq_ref, up_ref, ut_ref, h, total)
             if e < LEAPS:
                 u_all[1 - par, at(h, *st[h])] = place.astype(BF)
-        if e < LEAPS:
-            start_gather(1 - par)
+                start_gather(h, 1 - par)
+            else:
+                here = pl.ds(bs * h, bs)
+                stores.append(load(ut_ref.at[here], ut_out.at[here], 7 + h))
 
         vscatter1(0).wait_recv()
         each(lambda m: vscatter2(m).wait_recv(), others)
@@ -427,7 +459,9 @@
             place = advance(vq_ref, vp_ref, vt_ref, k, jnp.transpose(total))
             if e < LEAPS:
                 v_all[b] = place.astype(BF)
-        if e < LEAPS:
+        if e == LEAPS:
+            stores.append(load(vt_ref, vt_out, 9))
+        else:
             start_vgather()
             forward_gather(1 - par)
             forward_vgather()
@@ -436,6 +470,8 @@
             each(lambda m: scatter2(h, m).wait_send(), others)
         each(lambda m: vscatter1(m).wait_send(), everyone)
         each(lambda m: vscatter2(m).wait_send(), others)
+    for copy in stores:
+        copy.wait()
 
 
 def body(
@@ -447,8 +483,6 @@
     slots, bs = tile_values.shape[1], tile_values.shape[2]
     upairs = (slots + 2 * cols) // 2
     vpairs = (slots + 2 * rows) // 2
-    smem = pl.BlockSpec(memory_space=pltpu.SMEM)
-    vmem = pl.BlockSpec(memory_space=pltpu.VMEM)
     hbm = pl.BlockSpec(memory_space=pl.ANY)
     state = jax.ShapeDtypeStruct(compound_pos.shape, F32)
     sizes = (rows, cols, slots, bs, upairs, vpairs)
@@ -457,9 +491,13 @@
     out = pl.pallas_call(
         functools.partial(kernel, sizes),
         out_shape=(state,) * 6,
-        in_specs=[smem] + [vmem] * 6 + [hbm] * 2,
-        out_specs=(vmem,) * 6,
+        in_specs=[hbm] * 9,
+        out_specs=(hbm,) * 6,
         scratch_shapes=[
+            pltpu.SMEM((1,), I32),
+            pltpu.VMEM((1, slots), I32),
+            pltpu.VMEM((1, slots), I32),
+            *[pltpu.VMEM(compound_pos.shape, F32)] * 6,
             pltpu.VMEM((slots + 1, bs, bs), BF),
             pltpu.VMEM((slots + 1, bs, bs), BF),
             pltpu.VMEM((2 * upairs + 1, bs, bs), BF),
@@ -477,7 +515,7 @@
             pltpu.VMEM((SIDE, 2, bs, bs), BF),
             pltpu.VMEM((16, WIDTH), I32),
             pltpu.SMEM((16, WIDTH), I32),
-            dma((3,)),
+            dma((16,)),
             dma((full,)), dma((full,)), dma((step,)), dma((step,)),
             dma((step,)), dma((step,)), dma((full,)), dma((full,)),
             dma((SIDE,)), dma((SIDE,)), dma((SIDE,)), dma((SIDE,)),

time: 98.9 us -> 94.5 us (0.956)
  Pallas kernels: 95.4 us -> 91.1 us
    pallas_call x1, Pallas kernels: 95.4 us -> 91.1 us  [body(): pl.pallas_call(functools.partial(kernel, sizes), out_shape=(state,) * 6,...]
where the time goes in v4:
time: 94.5 us; the launch traced here: 94.4 us
  Pallas kernels  91.1 us (96%)
  other arithmetic  2.03 us (2%)
  between operations  1.29 us (1%)
    pallas_call x1, Pallas kernels, body(): pl.pallas_call(functools.partial(kernel, sizes), out_shape=(state,) * 6,...  91.1 us
    add x1, other arithmetic, body(): ends += [place, speed + 0.5 * EPS * (NU1 * total - LAMBDA * place)]  2.03 us

profile of v4, /device:TPU:1, one launch (start us, length us, event | category | flops | bytes accessed | tf_op | source)
XLA Modules:
  0.0 94.4 jit_solution(15278699759351603157)
XLA Ops:
  1.3 91.1 %shard_map.120 = (f32[256,128]{1,0:T(8,128)}, f32[256,128]{1,0:T(8,128)}, f32[256,128]{1,0:T(8,128)}, f32[256,128]{1,0:T(8,128)}, f32[256,128]{1,0:T(8,128)}, /*index=5*/f32[256,128]{1,0:T(8,128)}) custom-call(s32[1]{0:T(128)S(6)} %copy.13.count_hbm, s32[1,256]{1,0:T(1,128)} %trow_hbm.1, s32[1,256]{1,0:T(1,128)} %tcol_hbm.1, f32[256,128]{1,0:T(8,128)} %upos_hbm.1, ...), custom_call_target="tpu_custom_call" | custom-call | tf_op jit(solution)/shard_map/pallas_call | solution.py:491
  92.4 2.0 %multiply_add_fusion = (f32[256,128]{1,0:T(8,128)}, f32[256,128]{1,0:T(8,128)}, f32[256,128]{1,0:T(8,128)}, f32[256,128]{1,0:T(8,128)}) fusion(f32[256,128]{1,0:T(8,128)} %get-tuple-element.14, f32[256,128]{1,0:T(8,128)} %get-tuple-element.15, f32[256,128]{1,0:T(8,128)} %get-tuple-element.13, f32[256,128]{1,0:T(8,128)} %get-tuple-element.11, ...), kind=kLoop, calls=%fused_computation | loop fusion | flops 393216 | bytes 1310720 | tf_op jit(solution)/shard_map/add | solution.py:534
